TPU v7x, 32 devices: a whole 2x2x4 slice. The times are simulated.
32 devices in a mesh: grp: 2 (over x), chan: 16 (over z, y, core).
Axes of the slice: x: 2, y: 2, z: 4, core: 2. Of those that a mesh axis runs over, the one named last changes fastest.
Arguments:
- spectra: bfloat16 [1024, 2, 4, 4096], P(None, None, None, ('grp', 'chan')), parts along dimension 3, may hold values from -6 to 6
- quality: int32 [32, 4], P(('grp', 'chan')), parts along dimension 0, may hold values 0 or 1
Outputs:
- near_corr: bfloat16 [32, 9, 128, 128], P(('grp', 'chan')), parts along dimension 0
- far_corr: bfloat16 [32, 9, 128, 128], P(('grp', 'chan')), parts along dimension 0
There are 2 independent parts, one for each index of `grp`. A program takes and returns all parts, laid end to end along the dimension named above; each array names one. Nothing has to cross between parts.
All inputs are finite; a program needn't handle non-finite values. No bound on the sum of `quality` on one device may be relied on, other than what follows from the above.
Results may differ from a plain program's by a relative error of at most 0.012.
Values may be sent and summed in bfloat16 or wider, within the bound.
A program may use at most 64 MiB of HBM per device.

v0:
```python
import math

import jax
import jax.numpy as jnp
from jax import lax
from jax.experimental import pallas as pl
from jax.experimental.pallas import tpu as pltpu
from jax.sharding import PartitionSpec as P

HL = 4
LAGS = 2 * HL + 1
CHUNKS = 8
GROUPS = 3
GATE = 2
VMEM_LIMIT = 52 * 1024 * 1024


def lag_coeffs(first, width, freq_count, windows):
    col = first + lax.broadcasted_iota(jnp.int32, (1, width), 1)
    freq = lax.div(col, 2 * windows).astype(jnp.float32)
    sign = jnp.where(lax.rem(lax.div(col, windows), 2) == 0, -1.0, 1.0)
    y = (0.5 * freq_count - freq) * (math.pi / freq_count)
    square = y * y
    sine, cosine = jnp.zeros_like(y), jnp.zeros_like(y)
    for k in range(7, -1, -1):
        sine = sine * square + (-1.0) ** k / math.factorial(2 * k + 1)
        cosine = cosine * square + (-1.0) ** k / math.factorial(2 * k)
    c1, s1 = sine * y, cosine
    c2, s2 = 2.0 * c1 * c1 - 1.0, 2.0 * s1 * c1
    c3, s3 = c2 * c1 - s2 * s1, s2 * c1 + c2 * s1
    c4, s4 = 2.0 * c2 * c2 - 1.0, 2.0 * s2 * c2
    factor = 1.0 / math.sqrt(windows * freq_count)

    def rounded(value):
        return (value * factor).astype(jnp.bfloat16).astype(jnp.float32)

    cos = [rounded(v) for v in (jnp.ones_like(c1), c1, c2, c3, c4)]
    sin = [None] + [rounded(v * sign) for v in (s1, s2, s3, s4)]
    return cos, sin


def kernel(
    n,
    windows,
    quality_hbm,
    spec,
    near_out,
    far_out,
    own,
    near,
    far,
    extra,
    left,
    near_acc,
    far_acc,
    extra_acc,
    far_ret,
    near_ret,
    extra_buf,
    quality,
    my_mask,
    masks,
    load_sem,
    near_send,
    near_recv,
    far_send,
    far_recv,
    relay_send,
    extra_recv,
    mask_send,
    mask_recv,
    ret_send,
    ret_recv,
    xret_send,
    xret_recv,
    gate,
):
    me = lax.axis_index("chan")
    half = n // 2
    rows = spec.shape[0]
    chan = spec.shape[1]
    size = rows // CHUNKS
    before = lax.rem(me + n - 1, n)
    after = lax.rem(me + 1, n)
    across = lax.rem(me + half, n)
    low = lax.rem(me, half)
    rightward = lax.rem(lax.div(low, 2) + low, 2) == 0
    is_low = me < half
    sends_far = is_low == rightward
    takes_far = jnp.logical_not(sends_far)
    def from_low(p):
        return (p // 2 + p) % 2 == 0

    quarter = half // 2
    gates = []
    if half % 8 == 0 and from_low(quarter - 1) and from_low(quarter):
        gates += [(quarter - 1, n - 1), (quarter, half)]
    gated = me < 0
    for sender, _ in gates:
        gated = jnp.logical_or(gated, me == sender)
    near_here = me != half - 1
    relays = jnp.logical_or(me == half, me == n - 1)
    near_early = jnp.logical_and(near_here, jnp.logical_not(relays))

    def part(c):
        return pl.ds(pl.multiple_of(c * size, size), size)

    def remote(src, dst, send_sem, recv_sem, target):
        return pltpu.make_async_remote_copy(
            src_ref=src,
            dst_ref=dst,
            send_sem=send_sem,
            recv_sem=recv_sem,
            device_id={"chan": target},
            device_id_type=pl.DeviceIdType.MESH,
        )

    load_own = pltpu.make_async_copy(spec, own, load_sem.at[0])
    load_quality = pltpu.make_async_copy(quality_hbm, quality, load_sem.at[1])
    load_quality.start()
    load_own.start()

    barrier = pltpu.get_barrier_semaphore()
    offsets = (1, n - 1, half - 1, half, half + 1, quarter, n - quarter)
    for offset in offsets:
        pl.semaphore_signal(
            barrier,
            inc=1,
            device_id={"chan": lax.rem(me + offset, n)},
            device_id_type=pl.DeviceIdType.MESH,
        )
    pl.semaphore_wait(barrier, len(offsets))

    load_quality.wait()
    row = lax.rem(lax.broadcasted_iota(jnp.int32, (16, chan), 0), windows)
    flags = jnp.zeros((16, chan), jnp.int32)
    for w in range(windows):
        flags = jnp.where(row == w, quality[0, w], flags)
    my_mask[...] = flags.astype(jnp.float32).astype(jnp.bfloat16)

    def far_copy(c):
        return remote(spec.at[part(c)], far.at[part(c)], far_send.at[c], far_recv.at[c], across)

    def near_copy(c):
        return remote(spec.at[part(c)], near.at[part(c)], near_send.at[c], near_recv.at[c], before)

    def relay_to_near(c):
        return remote(far.at[part(c)], near.at[part(c)], relay_send.at[c], near_recv.at[c], n - 1)

    def relay_to_extra(c):
        return remote(far.at[part(c)], extra.at[part(c)], relay_send.at[c], extra_recv.at[c], half)

    def mask_copy(slot, target):
        return remote(my_mask, masks.at[slot], mask_send.at[slot], mask_recv.at[slot], target)

    mask_copies = [mask_copy(0, before), mask_copy(1, across), mask_copy(2, after)]
    for copy in mask_copies:
        copy.start()

    direct = jnp.logical_and(me != 0, me != half)

    @pl.loop(0, CHUNKS)
    def _(c):
        @pl.when(jnp.logical_and(sends_far, jnp.logical_not(gated)))
        def _():
            far_copy(c).start()

        @pl.when(direct)
        def _():
            near_copy(c).start()

    near_acc[...] = jnp.zeros_like(near_acc)
    far_acc[...] = jnp.zeros_like(far_acc)
    extra_acc[...] = jnp.zeros_like(extra_acc)

    load_own.wait()
    eye = (
        lax.broadcasted_iota(jnp.int32, (chan, chan), 0)
        == lax.broadcasted_iota(jnp.int32, (chan, chan), 1)
    ).astype(jnp.float32).astype(jnp.bfloat16)
    width = 256

    def turned(value):
        return lax.dot_general(
            eye, value, (((1,), (1,)), ((), ())), preferred_element_type=jnp.float32
        )

    def far_wait(c):
        @pl.when(jnp.logical_not(relays))
        def _():
            far_copy(c).wait_recv()

    def pass_on(c):
        far_copy(c).wait_recv()

        @pl.when(me == half)
        def _():
            relay_to_near(c).start()

        @pl.when(me == n - 1)
        def _():
            relay_to_extra(c).start()

        for sender, keeper in gates:

            @pl.when(jnp.logical_and(me == keeper, c == CHUNKS - GATE))
            def _():
                pl.semaphore_signal(
                    gate,
                    inc=1,
                    device_id={"chan": sender},
                    device_id_type=pl.DeviceIdType.MESH,
                )

    tiles = rows // width // CHUNKS

    @pl.loop(0, rows // width)
    def _(t):
        @pl.when(jnp.logical_and(relays, lax.rem(t, tiles) == tiles - 1))
        def _():
            pass_on(lax.div(t, tiles))

        cols = pl.ds(pl.multiple_of(t * width, width), width)
        block = own[cols, :]
        wide = block.astype(jnp.float32).reshape(width // 8, 8, chan)
        swapped = pltpu.roll(wide, 4, 1).reshape(width, chan).astype(jnp.bfloat16)
        straight = turned(block)
        crossed = turned(swapped)
        cos, sin = lag_coeffs(t * width, width, rows // (2 * windows), windows)
        left[pl.ds(HL * chan, chan), cols] = (straight * cos[0]).astype(jnp.bfloat16)
        for lag in range(1, HL + 1):
            a = straight * cos[lag]
            b = crossed * sin[lag]
            left[pl.ds((HL + lag) * chan, chan), cols] = (a + b).astype(jnp.bfloat16)
            left[pl.ds((HL - lag) * chan, chan), cols] = (a - b).astype(jnp.bfloat16)

    @pl.when(gated)
    def _():
        pl.semaphore_wait(gate, 1)

        @pl.loop(0, CHUNKS)
        def _(c):
            far_copy(c).start()

    for copy in mask_copies:
        copy.wait()

    def masked(ref, slot, c):
        both = my_mask[...] * masks[slot]
        return (ref[part(c), :].reshape(size // 16, 16, chan) * both[None]).reshape(size, chan)

    def add(acc, ref, slot, c):
        acc[...] += jnp.dot(
            left[:, part(c)], masked(ref, slot, c), preferred_element_type=jnp.float32
        )

    def near_step(c):
        near_copy(c).wait_recv()
        add(near_acc, near, 0, c)

    def extra_step(c):
        relay_to_extra(c).wait_recv()
        add(extra_acc, extra, 2, c)

    @pl.loop(0, CHUNKS - 1)
    def _(c):
        @pl.when(takes_far)
        def _():
            far_wait(c)
            add(far_acc, far, 1, c)

        @pl.when(jnp.logical_and(c > 0, near_early))
        def _():
            near_step(c - 1)

    @pl.when(near_early)
    def _():
        near_step(CHUNKS - 2)

    band = LAGS * chan // GROUPS
    last = CHUNKS - 1

    def ret_copy(g):
        span = pl.ds(g * band, band)
        return remote(far_out.at[span], far_ret.at[span], ret_send.at[g], ret_recv.at[g], across)

    def xret_copy():
        return remote(extra_buf, near_ret, xret_send, xret_recv, half - 1)

    @pl.when(takes_far)
    def _():
        far_wait(last)
        right = masked(far, 1, last)
        for g in range(GROUPS):
            span = pl.ds(g * band, band)
            far_out[span, :] = (
                far_acc[span, :]
                + jnp.dot(left[span, part(last)], right, preferred_element_type=jnp.float32)
            ).astype(jnp.bfloat16)
            ret_copy(g).start()

    @pl.when(near_early)
    def _():
        near_step(last)

    @pl.when(relays)
    def _():
        @pl.loop(0, CHUNKS)
        def _(c):
            near_step(c)

    @pl.when(me == half)
    def _():
        @pl.loop(0, CHUNKS)
        def _(c):
            extra_step(c)

    @pl.when(near_here)
    def _():
        near_out[...] = near_acc[...].astype(jnp.bfloat16)

    @pl.when(me == half)
    def _():
        extra_buf[...] = extra_acc[...].astype(jnp.bfloat16)
        xret_copy().start()

    def flip(src, dst, lag):
        tile = src[pl.ds((LAGS - 1 - lag) * chan, chan), :].astype(jnp.float32)
        dst[pl.ds(lag * chan, chan), :] = tile.T.astype(jnp.bfloat16)

    per = LAGS // GROUPS

    @pl.when(sends_far)
    def _():
        for g in range(GROUPS):
            ret_copy(g).wait_recv()
            for k in range(per):
                flip(far_ret, far_out, LAGS - 1 - (g * per + k))

    @pl.when(me == half - 1)
    def _():
        xret_copy().wait_recv()
        for lag in range(LAGS):
            flip(near_ret, near_out, lag)

    @pl.loop(0, CHUNKS)
    def _(c):
        @pl.when(sends_far)
        def _():
            far_copy(c).wait_send()

        @pl.when(direct)
        def _():
            near_copy(c).wait_send()

        @pl.when(jnp.logical_or(me == half, me == n - 1))
        def _():
            relay_to_near(c).wait_send()

    @pl.when(takes_far)
    def _():
        for g in range(GROUPS):
            ret_copy(g).wait_send()

    @pl.when(me == half)
    def _():
        xret_copy().wait_send()


def local(spectra, quality):
    n = lax.axis_size("chan")
    freq_count, parts, windows, chan = spectra.shape
    rows = freq_count * parts * windows
    out = jax.ShapeDtypeStruct((LAGS * chan, chan), jnp.bfloat16)
    block = pltpu.VMEM((rows, chan), jnp.bfloat16)
    acc = pltpu.VMEM((LAGS * chan, chan), jnp.float32)
    result = pltpu.VMEM((LAGS * chan, chan), jnp.bfloat16)
    dma = pltpu.SemaphoreType.DMA
    near, far = pl.pallas_call(
        lambda *refs: kernel(n, windows, *refs),
        out_shape=(out, out),
        in_specs=[
            pl.BlockSpec(memory_space=pl.ANY),
            pl.BlockSpec(memory_space=pl.ANY),
        ],
        out_specs=(pl.BlockSpec(memory_space=pltpu.VMEM), pl.BlockSpec(memory_space=pltpu.VMEM)),
        scratch_shapes=[
            block,
            block,
            block,
            block,
            pltpu.VMEM((LAGS * chan, rows), jnp.bfloat16),
            acc,
            acc,
            acc,
            result,
            result,
            result,
            pltpu.SMEM((1, windows), jnp.int32),
            pltpu.VMEM((16, chan), jnp.bfloat16),
            pltpu.VMEM((3, 16, chan), jnp.bfloat16),
            dma((2,)),
            dma((CHUNKS,)),
            dma((CHUNKS,)),
            dma((CHUNKS,)),
            dma((CHUNKS,)),
            dma((CHUNKS,)),
            dma((CHUNKS,)),
            dma((3,)),
            dma((3,)),
            dma((GROUPS,)),
            dma((GROUPS,)),
            dma(()),
            dma(()),
            pltpu.SemaphoreType.REGULAR,
        ],
        compiler_params=pltpu.CompilerParams(
            collective_id=0, has_side_effects=True, vmem_limit_bytes=VMEM_LIMIT
        ),
        name="lag_correlation",
    )(quality, spectra.reshape(rows, chan))
    shape = (1, LAGS, chan, chan)
    return near.reshape(shape), far.reshape(shape)


def solution(mesh):
    return jax.shard_map(
        local,
        mesh=mesh,
        in_specs=(P(None, None, None, ("grp", "chan")), P(("grp", "chan"), None)),
        out_specs=(P(("grp", "chan"), None, None, None), P(("grp", "chan"), None, None, None)),
        check_vma=False,
    )
```

profile of v0, /device:TPU:13, one launch (start us, length us, event | category | flops | bytes accessed | tf_op | source)
XLA Modules:
  0.0 63.7 jit_solution(8085026975850044000)
XLA Ops:
  0.6 0.0 copy-start
  0.6 0.6 %copy-done = s32[1,4]{1,0:T(1,128)S(1)} copy-done((s32[1,4]{1,0:T(1,128)S(1)}, s32[1,4]{1,0:T(1,128)}, u32[]{:S(2)}) %copy-start) | copy-done | bytes 40
  1.3 60.9 %lag_correlation.1 = (bf16[1152,128]{1,0:T(8,128)(2,1)S(1)}, bf16[1152,128]{1,0:T(8,128)(2,1)S(1)}) custom-call(s32[1,4]{1,0:T(1,128)S(1)} %copy-done, bf16[8192,128]{1,0:T(8,128)(2,1)} %bitcast.5), custom_call_target="tpu_custom_call" | custom-call | tf_op jit(solution)/shard_map/lag_correlation/pallas_call | solution.py:379
  62.2 0.7 %copy.6 = bf16[1,9,128,128]{3,2,1,0:T(8,128)(2,1)} copy(bf16[1,9,128,128]{3,2,1,0:T(8,128)(2,1)S(1)} %bitcast.4) | data formatting | bytes 589824
  62.9 0.7 %copy.7 = bf16[1,9,128,128]{3,2,1,0:T(8,128)(2,1)} copy(bf16[1,9,128,128]{3,2,1,0:T(8,128)(2,1)S(1)} %bitcast.3) | data formatting | bytes 589824
Async XLA Ops:
  0.6 0.7 %copy-start = (s32[1,4]{1,0:T(1,128)S(1)}, s32[1,4]{1,0:T(1,128)}, u32[]{:S(2)}) copy-start(s32[1,4]{1,0:T(1,128)} %refs_0_.1) | copy-start | bytes 52
where the time goes:
time: 63.8 us; the launch traced here: 63.7 us
  Pallas kernels  60.9 us (95%)
  local copies, waits for them, and re-layouts  2.08 us (3%)
  between operations  0.65 us (1%)
    pallas_call x1, Pallas kernels, local(): pl.pallas_call(lambda *refs: kernel(n, windows, *refs), out_shape=(out, o...  60.9 us
    unnamed x4, local copies, waits for them, and re-layouts  2.08 us

commit v1 on v0

--- a/solution.py
+++ b/solution.py
@@ -58,8 +58,6 @@
     near_ret,
     extra_buf,
     quality,
-    my_mask,
-    masks,
     load_sem,
     near_send,
     near_recv,
@@ -67,8 +65,6 @@
     far_recv,
     relay_send,
     extra_recv,
-    mask_send,
-    mask_recv,
     ret_send,
     ret_recv,
     xret_send,
@@ -115,49 +111,75 @@
             device_id_type=pl.DeviceIdType.MESH,
         )
 
-    load_own = pltpu.make_async_copy(spec, own, load_sem.at[0])
-    load_quality = pltpu.make_async_copy(quality_hbm, quality, load_sem.at[1])
+    def load_own(c):
+        return pltpu.make_async_copy(spec.at[part(c)], own.at[part(c)], load_sem.at[c])
+
+    load_quality = pltpu.make_async_copy(quality_hbm, quality, load_sem.at[CHUNKS])
     load_quality.start()
-    load_own.start()
-
+
+    @pl.loop(0, CHUNKS)
+    def _(c):
+        load_own(c).start()
+
+    direct = jnp.logical_and(me != 0, me != half)
     barrier = pltpu.get_barrier_semaphore()
-    offsets = (1, n - 1, half - 1, half, half + 1, quarter, n - quarter)
-    for offset in offsets:
+
+    def greet(target):
         pl.semaphore_signal(
-            barrier,
-            inc=1,
-            device_id={"chan": lax.rem(me + offset, n)},
-            device_id_type=pl.DeviceIdType.MESH,
+            barrier, inc=1, device_id={"chan": target}, device_id_type=pl.DeviceIdType.MESH
         )
-    pl.semaphore_wait(barrier, len(offsets))
+
+    greet(across)
+
+    @pl.when(jnp.logical_and(me != half - 1, me != n - 1))
+    def _():
+        greet(after)
+
+    @pl.when(me == half)
+    def _():
+        greet(n - 1)
+
+    @pl.when(jnp.logical_or(me == n - 1, me == half - 1))
+    def _():
+        greet(half)
+
+    for sender, keeper in gates:
+
+        @pl.when(me == sender)
+        def _():
+            greet(keeper)
+
+    expected = 1 + jnp.where(direct, 1, 0)
+    expected += jnp.where(me == half, 2, 0) + jnp.where(me == n - 1, 1, 0)
+    for _, keeper in gates:
+        expected += jnp.where(me == keeper, 1, 0)
 
     load_quality.wait()
     row = lax.rem(lax.broadcasted_iota(jnp.int32, (16, chan), 0), windows)
     flags = jnp.zeros((16, chan), jnp.int32)
     for w in range(windows):
         flags = jnp.where(row == w, quality[0, w], flags)
-    my_mask[...] = flags.astype(jnp.float32).astype(jnp.bfloat16)
+    mask = flags.astype(jnp.float32).astype(jnp.bfloat16)
+
+    @pl.loop(0, CHUNKS)
+    def _(c):
+        load_own(c).wait()
+        block = own[part(c), :].reshape(size // 16, 16, chan)
+        own[part(c), :] = (block * mask[None]).reshape(size, chan)
+
+    pl.semaphore_wait(barrier, expected)
 
     def far_copy(c):
-        return remote(spec.at[part(c)], far.at[part(c)], far_send.at[c], far_recv.at[c], across)
+        return remote(own.at[part(c)], far.at[part(c)], far_send.at[c], far_recv.at[c], across)
 
     def near_copy(c):
-        return remote(spec.at[part(c)], near.at[part(c)], near_send.at[c], near_recv.at[c], before)
+        return remote(own.at[part(c)], near.at[part(c)], near_send.at[c], near_recv.at[c], before)
 
     def relay_to_near(c):
         return remote(far.at[part(c)], near.at[part(c)], relay_send.at[c], near_recv.at[c], n - 1)
 
     def relay_to_extra(c):
         return remote(far.at[part(c)], extra.at[part(c)], relay_send.at[c], extra_recv.at[c], half)
-
-    def mask_copy(slot, target):
-        return remote(my_mask, masks.at[slot], mask_send.at[slot], mask_recv.at[slot], target)
-
-    mask_copies = [mask_copy(0, before), mask_copy(1, across), mask_copy(2, after)]
-    for copy in mask_copies:
-        copy.start()
-
-    direct = jnp.logical_and(me != 0, me != half)
 
     @pl.loop(0, CHUNKS)
     def _(c):
@@ -173,7 +195,6 @@
     far_acc[...] = jnp.zeros_like(far_acc)
     extra_acc[...] = jnp.zeros_like(extra_acc)
 
-    load_own.wait()
     eye = (
         lax.broadcasted_iota(jnp.int32, (chan, chan), 0)
         == lax.broadcasted_iota(jnp.int32, (chan, chan), 1)
@@ -242,32 +263,25 @@
         def _(c):
             far_copy(c).start()
 
-    for copy in mask_copies:
-        copy.wait()
-
-    def masked(ref, slot, c):
-        both = my_mask[...] * masks[slot]
-        return (ref[part(c), :].reshape(size // 16, 16, chan) * both[None]).reshape(size, chan)
-
-    def add(acc, ref, slot, c):
+    def add(acc, ref, c):
         acc[...] += jnp.dot(
-            left[:, part(c)], masked(ref, slot, c), preferred_element_type=jnp.float32
+            left[:, part(c)], ref[part(c), :], preferred_element_type=jnp.float32
         )
 
     def near_step(c):
         near_copy(c).wait_recv()
-        add(near_acc, near, 0, c)
+        add(near_acc, near, c)
 
     def extra_step(c):
         relay_to_extra(c).wait_recv()
-        add(extra_acc, extra, 2, c)
+        add(extra_acc, extra, c)
 
     @pl.loop(0, CHUNKS - 1)
     def _(c):
         @pl.when(takes_far)
         def _():
             far_wait(c)
-            add(far_acc, far, 1, c)
+            add(far_acc, far, c)
 
         @pl.when(jnp.logical_and(c > 0, near_early))
         def _():
@@ -290,7 +304,7 @@
     @pl.when(takes_far)
     def _():
         far_wait(last)
-        right = masked(far, 1, last)
+        right = far[part(last), :]
         for g in range(GROUPS):
             span = pl.ds(g * band, band)
             far_out[span, :] = (
@@ -365,6 +379,17 @@
     @pl.when(me == half)
     def _():
         xret_copy().wait_send()
+
+
+def store_results(near, far, near_out, far_out, sems):
+    copies = [
+        pltpu.make_async_copy(near, near_out, sems.at[0]),
+        pltpu.make_async_copy(far, far_out, sems.at[1]),
+    ]
+    for copy in copies:
+        copy.start()
+    for copy in copies:
+        copy.wait()
 
 
 def local(spectra, quality):
@@ -397,17 +422,13 @@
             result,
             result,
             pltpu.SMEM((1, windows), jnp.int32),
-            pltpu.VMEM((16, chan), jnp.bfloat16),
-            pltpu.VMEM((3, 16, chan), jnp.bfloat16),
-            dma((2,)),
-            dma((CHUNKS,)),
-            dma((CHUNKS,)),
-            dma((CHUNKS,)),
-            dma((CHUNKS,)),
-            dma((CHUNKS,)),
-            dma((CHUNKS,)),
-            dma((3,)),
-            dma((3,)),
+            dma((CHUNKS + 1,)),
+            dma((CHUNKS,)),
+            dma((CHUNKS,)),
+            dma((CHUNKS,)),
+            dma((CHUNKS,)),
+            dma((CHUNKS,)),
+            dma((CHUNKS,)),
             dma((GROUPS,)),
             dma((GROUPS,)),
             dma(()),
@@ -419,6 +440,15 @@
         ),
         name="lag_correlation",
     )(quality, spectra.reshape(rows, chan))
+    near, far = pl.pallas_call(
+        store_results,
+        out_shape=(out, out),
+        in_specs=[pl.BlockSpec(memory_space=pl.ANY)] * 2,
+        out_specs=[pl.BlockSpec(memory_space=pl.ANY)] * 2,
+        scratch_shapes=[dma((2,))],
+        compiler_params=pltpu.CompilerParams(vmem_limit_bytes=1024 * 1024),
+        name="store_results",
+    )(near, far)
     shape = (1, LAGS, chan, chan)
     return near.reshape(shape), far.reshape(shape)
 

time: 63.8 us -> 63.9 us (level)
  Pallas kernels: 60.9 us -> 62.4 us
  local copies, waits for them, and re-layouts: 2.08 us -> 0.65 us
    unnamed x4 -> x2, local copies, waits for them, and re-layouts: 2.08 us -> 0.65 us
    pallas_call x0 -> x1, Pallas kernels: none -> 0.83 us  [local(): pl.pallas_call(store_results, out_shape=(out, out), in_specs=[pl.BlockSpe...]
    pallas_call x1, Pallas kernels: 60.9 us -> 61.6 us  [local(): pl.pallas_call(lambda *refs: kernel(n, windows, *refs), out_shape=(out, o...]
where the time goes in v1:
time: 63.9 us; the launch traced here: 63.7 us
  Pallas kernels  62.4 us (98%)
  local copies, waits for them, and re-layouts  0.65 us (1%)
  between operations  0.65 us (1%)
    pallas_call x1, Pallas kernels, local(): pl.pallas_call(lambda *refs: kernel(n, windows, *refs), out_shape=(out, o...  61.6 us

profile of v1, /device:TPU:13, one launch (start us, length us, event | category | flops | bytes accessed | tf_op | source)
XLA Modules:
  0.0 63.7 jit_solution(11793312766678035924)
XLA Ops:
  0.6 0.0 copy-start
  0.6 0.6 %copy-done = s32[1,4]{1,0:T(1,128)S(1)} copy-done((s32[1,4]{1,0:T(1,128)S(1)}, s32[1,4]{1,0:T(1,128)}, u32[]{:S(2)}) %copy-start) | copy-done | bytes 40
  1.3 61.6 %lag_correlation.1 = (bf16[1152,128]{1,0:T(8,128)(2,1)S(1)}, bf16[1152,128]{1,0:T(8,128)(2,1)S(1)}) custom-call(s32[1,4]{1,0:T(1,128)S(1)} %copy-done, bf16[8192,128]{1,0:T(8,128)(2,1)} %bitcast.3), custom_call_target="tpu_custom_call" | custom-call | tf_op jit(solution)/shard_map/lag_correlation/pallas_call | solution.py:404
  62.9 0.8 %store_results.1 = (bf16[1152,128]{1,0:T(8,128)(2,1)}, bf16[1152,128]{1,0:T(8,128)(2,1)}) custom-call(bf16[1152,128]{1,0:T(8,128)(2,1)S(1)} %get-tuple-element.6.near, bf16[1152,128]{1,0:T(8,128)(2,1)S(1)} %get-tuple-element.7.far), custom_call_target="tpu_custom_call" | custom-call | tf_op jit(solution)/shard_map/store_results/pallas_call | solution.py:443
Async XLA Ops:
  0.6 0.7 %copy-start = (s32[1,4]{1,0:T(1,128)S(1)}, s32[1,4]{1,0:T(1,128)}, u32[]{:S(2)}) copy-start(s32[1,4]{1,0:T(1,128)} %refs_0_.1) | copy-start | bytes 52

commit v2 on v1

--- a/solution.py
+++ b/solution.py
@@ -70,6 +70,7 @@
     xret_send,
     xret_recv,
     gate,
+    mate_sent,
 ):
     me = lax.axis_index("chan")
     half = n // 2
@@ -79,6 +80,7 @@
     before = lax.rem(me + n - 1, n)
     after = lax.rem(me + 1, n)
     across = lax.rem(me + half, n)
+    mate = me + 1 - 2 * lax.rem(me, 2)
     low = lax.rem(me, half)
     rightward = lax.rem(lax.div(low, 2) + low, 2) == 0
     is_low = me < half
@@ -89,8 +91,10 @@
 
     quarter = half // 2
     gates = []
-    if half % 8 == 0 and from_low(quarter - 1) and from_low(quarter):
-        gates += [(quarter - 1, n - 1), (quarter, half)]
+    if half % 8 == 0 and from_low(quarter - 1):
+        gates += [(quarter - 1, n - 1)]
+    if not from_low(half - 2):
+        gates += [(n - 2, n - 1)]
     gated = me < 0
     for sender, _ in gates:
         gated = jnp.logical_or(gated, me == sender)
@@ -131,6 +135,10 @@
 
     greet(across)
 
+    @pl.when(takes_far)
+    def _():
+        greet(mate)
+
     @pl.when(jnp.logical_and(me != half - 1, me != n - 1))
     def _():
         greet(after)
@@ -149,7 +157,7 @@
         def _():
             greet(keeper)
 
-    expected = 1 + jnp.where(direct, 1, 0)
+    expected = 1 + jnp.where(direct, 1, 0) + jnp.where(sends_far, 1, 0)
     expected += jnp.where(me == half, 2, 0) + jnp.where(me == n - 1, 1, 0)
     for _, keeper in gates:
         expected += jnp.where(me == keeper, 1, 0)
@@ -290,6 +298,16 @@
     @pl.when(near_early)
     def _():
         near_step(CHUNKS - 2)
+        near_step(CHUNKS - 1)
+
+    @pl.when(me == half)
+    def _():
+        @pl.loop(0, CHUNKS)
+        def _(c):
+            near_step(c)
+            extra_step(c)
+
+        extra_buf[...] = extra_acc[...].astype(jnp.bfloat16)
 
     band = LAGS * chan // GROUPS
     last = CHUNKS - 1
@@ -304,6 +322,7 @@
     @pl.when(takes_far)
     def _():
         far_wait(last)
+        pl.semaphore_wait(mate_sent, 1)
         right = far[part(last), :]
         for g in range(GROUPS):
             span = pl.ds(g * band, band)
@@ -313,30 +332,29 @@
             ).astype(jnp.bfloat16)
             ret_copy(g).start()
 
-    @pl.when(near_early)
-    def _():
-        near_step(last)
-
-    @pl.when(relays)
+    @pl.when(me == half)
+    def _():
+        xret_copy().start()
+
+    @pl.when(me == n - 1)
     def _():
         @pl.loop(0, CHUNKS)
         def _(c):
             near_step(c)
 
-    @pl.when(me == half)
+    @pl.when(near_here)
+    def _():
+        near_out[...] = near_acc[...].astype(jnp.bfloat16)
+
+    @pl.when(sends_far)
     def _():
         @pl.loop(0, CHUNKS)
         def _(c):
-            extra_step(c)
-
-    @pl.when(near_here)
-    def _():
-        near_out[...] = near_acc[...].astype(jnp.bfloat16)
-
-    @pl.when(me == half)
-    def _():
-        extra_buf[...] = extra_acc[...].astype(jnp.bfloat16)
-        xret_copy().start()
+            far_copy(c).wait_send()
+
+        pl.semaphore_signal(
+            mate_sent, inc=1, device_id={"chan": mate}, device_id_type=pl.DeviceIdType.MESH
+        )
 
     def flip(src, dst, lag):
         tile = src[pl.ds((LAGS - 1 - lag) * chan, chan), :].astype(jnp.float32)
@@ -359,10 +377,6 @@
 
     @pl.loop(0, CHUNKS)
     def _(c):
-        @pl.when(sends_far)
-        def _():
-            far_copy(c).wait_send()
-
         @pl.when(direct)
         def _():
             near_copy(c).wait_send()
@@ -434,6 +448,7 @@
             dma(()),
             dma(()),
             pltpu.SemaphoreType.REGULAR,
+            pltpu.SemaphoreType.REGULAR,
         ],
         compiler_params=pltpu.CompilerParams(
             collective_id=0, has_side_effects=True, vmem_limit_bytes=VMEM_LIMIT

time: 63.9 us -> 66.8 us (1.045)
  Pallas kernels: 62.4 us -> 65.4 us
    pallas_call x1, Pallas kernels: 61.6 us -> 64.5 us  [local(): pl.pallas_call(lambda *refs: kernel(n, windows, *refs), out_shape=(out, o...]
where the time goes in v2:
time: 66.8 us; the launch traced here: 66.7 us
  Pallas kernels  65.4 us (98%)
    pallas_call x1, Pallas kernels, local(): pl.pallas_call(lambda *refs: kernel(n, windows, *refs), out_shape=(out, o...  64.5 us

profile of v2, /device:TPU:13, one launch (start us, length us, event | category | flops | bytes accessed | tf_op | source)
XLA Modules:
  0.0 66.7 jit_solution(5446583458607541223)
XLA Ops:
  0.6 0.0 copy-start
  0.6 0.6 copy-done
  1.3 64.5 %lag_correlation.1 = (bf16[1152,128]{1,0:T(8,128)(2,1)S(1)}, bf16[1152,128]{1,0:T(8,128)(2,1)S(1)}) custom-call(s32[1,4]{1,0:T(1,128)S(1)} %copy-done, bf16[8192,128]{1,0:T(8,128)(2,1)} %bitcast.3), custom_call_target="tpu_custom_call" | custom-call | tf_op jit(solution)/shard_map/lag_correlation/pallas_call | solution.py:418
  65.8 0.8 %store_results.1 = (bf16[1152,128]{1,0:T(8,128)(2,1)}, bf16[1152,128]{1,0:T(8,128)(2,1)}) custom-call(bf16[1152,128]{1,0:T(8,128)(2,1)S(1)} %get-tuple-element.6.near, bf16[1152,128]{1,0:T(8,128)(2,1)S(1)} %get-tuple-element.7.far), custom_call_target="tpu_custom_call" | custom-call | tf_op jit(solution)/shard_map/store_results/pallas_call | solution.py:458
Async XLA Ops:
  0.6 0.7 copy-start

commit v3 on v2

--- a/solution.py
+++ b/solution.py
@@ -11,7 +11,8 @@
 LAGS = 2 * HL + 1
 CHUNKS = 8
 GROUPS = 3
-GATE = 2
+FIRST = 4
+EARLY = 5
 VMEM_LIMIT = 52 * 1024 * 1024
 
 
@@ -82,22 +83,17 @@
     across = lax.rem(me + half, n)
     mate = me + 1 - 2 * lax.rem(me, 2)
     low = lax.rem(me, half)
-    rightward = lax.rem(lax.div(low, 2) + low, 2) == 0
+    pair = lax.div(low, 2)
+    mixed = lax.rem(pair, 2) == 0
+    rightward = jnp.logical_or(
+        jnp.logical_and(mixed, lax.rem(low, 2) == 0), lax.rem(pair, 4) == 3
+    )
     is_low = me < half
     sends_far = is_low == rightward
     takes_far = jnp.logical_not(sends_far)
-    def from_low(p):
-        return (p // 2 + p) % 2 == 0
-
-    quarter = half // 2
-    gates = []
-    if half % 8 == 0 and from_low(quarter - 1):
-        gates += [(quarter - 1, n - 1)]
-    if not from_low(half - 2):
-        gates += [(n - 2, n - 1)]
-    gated = me < 0
-    for sender, _ in gates:
-        gated = jnp.logical_or(gated, me == sender)
+    gated = me == half - 2
+    holds_back = jnp.logical_or(jnp.logical_and(takes_far, mixed), me == n - 1)
+    frees_mate = jnp.logical_and(sends_far, mixed)
     near_here = me != half - 1
     relays = jnp.logical_or(me == half, me == n - 1)
     near_early = jnp.logical_and(near_here, jnp.logical_not(relays))
@@ -135,10 +131,18 @@
 
     greet(across)
 
-    @pl.when(takes_far)
+    @pl.when(jnp.logical_and(takes_far, mixed))
     def _():
         greet(mate)
 
+    @pl.when(me == n - 1)
+    def _():
+        greet(n - 5)
+
+    @pl.when(gated)
+    def _():
+        greet(half - 1)
+
     @pl.when(jnp.logical_and(me != half - 1, me != n - 1))
     def _():
         greet(after)
@@ -151,16 +155,9 @@
     def _():
         greet(half)
 
-    for sender, keeper in gates:
-
-        @pl.when(me == sender)
-        def _():
-            greet(keeper)
-
-    expected = 1 + jnp.where(direct, 1, 0) + jnp.where(sends_far, 1, 0)
+    expected = 1 + jnp.where(direct, 1, 0) + jnp.where(frees_mate, 1, 0)
     expected += jnp.where(me == half, 2, 0) + jnp.where(me == n - 1, 1, 0)
-    for _, keeper in gates:
-        expected += jnp.where(me == keeper, 1, 0)
+    expected += jnp.where(jnp.logical_or(me == half - 1, me == n - 5), 1, 0)
 
     load_quality.wait()
     row = lax.rem(lax.broadcasted_iota(jnp.int32, (16, chan), 0), windows)
@@ -178,16 +175,23 @@
     pl.semaphore_wait(barrier, expected)
 
     def far_copy(c):
-        return remote(own.at[part(c)], far.at[part(c)], far_send.at[c], far_recv.at[c], across)
+        sent = far_send.at[lax.div(c, FIRST)]
+        return remote(own.at[part(c)], far.at[part(c)], sent, far_recv.at[c], across)
 
     def near_copy(c):
-        return remote(own.at[part(c)], near.at[part(c)], near_send.at[c], near_recv.at[c], before)
+        return remote(own.at[part(c)], near.at[part(c)], near_send, near_recv.at[c], before)
 
     def relay_to_near(c):
-        return remote(far.at[part(c)], near.at[part(c)], relay_send.at[c], near_recv.at[c], n - 1)
+        return remote(far.at[part(c)], near.at[part(c)], relay_send, near_recv.at[c], n - 1)
 
     def relay_to_extra(c):
-        return remote(far.at[part(c)], extra.at[part(c)], relay_send.at[c], extra_recv.at[c], half)
+        return remote(far.at[part(c)], extra.at[part(c)], relay_send, extra_recv.at[c], half)
+
+    def far_sent(group):
+        span = pl.ds(group * FIRST * size, FIRST * size)
+        remote(
+            own.at[span], far.at[span], far_send.at[group], far_recv.at[0], across
+        ).wait_send()
 
     @pl.loop(0, CHUNKS)
     def _(c):
@@ -229,17 +233,6 @@
         @pl.when(me == n - 1)
         def _():
             relay_to_extra(c).start()
-
-        for sender, keeper in gates:
-
-            @pl.when(jnp.logical_and(me == keeper, c == CHUNKS - GATE))
-            def _():
-                pl.semaphore_signal(
-                    gate,
-                    inc=1,
-                    device_id={"chan": sender},
-                    device_id_type=pl.DeviceIdType.MESH,
-                )
 
     tiles = rows // width // CHUNKS
 
@@ -263,6 +256,13 @@
             left[pl.ds((HL + lag) * chan, chan), cols] = (a + b).astype(jnp.bfloat16)
             left[pl.ds((HL - lag) * chan, chan), cols] = (a - b).astype(jnp.bfloat16)
 
+    @pl.when(me == half - 1)
+    def _():
+        far_sent(0)
+        pl.semaphore_signal(
+            gate, inc=1, device_id={"chan": half - 2}, device_id_type=pl.DeviceIdType.MESH
+        )
+
     @pl.when(gated)
     def _():
         pl.semaphore_wait(gate, 1)
@@ -309,6 +309,12 @@
 
         extra_buf[...] = extra_acc[...].astype(jnp.bfloat16)
 
+    @pl.when(me == n - 1)
+    def _():
+        @pl.loop(0, EARLY)
+        def _(c):
+            near_step(c)
+
     band = LAGS * chan // GROUPS
     last = CHUNKS - 1
 
@@ -322,7 +328,11 @@
     @pl.when(takes_far)
     def _():
         far_wait(last)
-        pl.semaphore_wait(mate_sent, 1)
+
+        @pl.when(holds_back)
+        def _():
+            pl.semaphore_wait(mate_sent, 1)
+
         right = far[part(last), :]
         for g in range(GROUPS):
             span = pl.ds(g * band, band)
@@ -338,7 +348,7 @@
 
     @pl.when(me == n - 1)
     def _():
-        @pl.loop(0, CHUNKS)
+        @pl.loop(EARLY, CHUNKS)
         def _(c):
             near_step(c)
 
@@ -346,15 +356,26 @@
     def _():
         near_out[...] = near_acc[...].astype(jnp.bfloat16)
 
+    def free(target):
+        pl.semaphore_signal(
+            mate_sent, inc=1, device_id={"chan": target}, device_id_type=pl.DeviceIdType.MESH
+        )
+
     @pl.when(sends_far)
     def _():
-        @pl.loop(0, CHUNKS)
-        def _(c):
-            far_copy(c).wait_send()
-
-        pl.semaphore_signal(
-            mate_sent, inc=1, device_id={"chan": mate}, device_id_type=pl.DeviceIdType.MESH
-        )
+        @pl.when(me != half - 1)
+        def _():
+            far_sent(0)
+
+        far_sent(1)
+
+        @pl.when(mixed)
+        def _():
+            free(mate)
+
+        @pl.when(me == n - 5)
+        def _():
+            free(n - 1)
 
     def flip(src, dst, lag):
         tile = src[pl.ds((LAGS - 1 - lag) * chan, chan), :].astype(jnp.float32)
@@ -375,15 +396,13 @@
         for lag in range(LAGS):
             flip(near_ret, near_out, lag)
 
-    @pl.loop(0, CHUNKS)
-    def _(c):
-        @pl.when(direct)
-        def _():
-            near_copy(c).wait_send()
-
-        @pl.when(jnp.logical_or(me == half, me == n - 1))
-        def _():
-            relay_to_near(c).wait_send()
+    @pl.when(direct)
+    def _():
+        remote(own, near, near_send, near_recv.at[0], before).wait_send()
+
+    @pl.when(relays)
+    def _():
+        remote(far, near, relay_send, near_recv.at[0], n - 1 + half - me).wait_send()
 
     @pl.when(takes_far)
     def _():
@@ -437,11 +456,11 @@
             result,
             pltpu.SMEM((1, windows), jnp.int32),
             dma((CHUNKS + 1,)),
+            dma(()),
             dma((CHUNKS,)),
+            dma((CHUNKS // FIRST,)),
             dma((CHUNKS,)),
-            dma((CHUNKS,)),
-            dma((CHUNKS,)),
-            dma((CHUNKS,)),
+            dma(()),
             dma((CHUNKS,)),
             dma((GROUPS,)),
             dma((GROUPS,)),

time: 66.8 us -> 66.6 us (level)
  no operation moved by 1% of the time
where the time goes in v3:
time: 66.6 us; the launch traced here: 66.4 us
  Pallas kernels  65.1 us (98%)
    pallas_call x1, Pallas kernels, local(): pl.pallas_call(lambda *refs: kernel(n, windows, *refs), out_shape=(out, o...  64.3 us

profile of v3, /device:TPU:13, one launch (start us, length us, event | category | flops | bytes accessed | tf_op | source)
XLA Modules:
  0.0 66.4 jit_solution(15292079800971685185)
XLA Ops:
  0.6 0.0 copy-start
  0.6 0.6 copy-done
  1.3 64.3 %lag_correlation.1 = (bf16[1152,128]{1,0:T(8,128)(2,1)S(1)}, bf16[1152,128]{1,0:T(8,128)(2,1)S(1)}) custom-call(s32[1,4]{1,0:T(1,128)S(1)} %copy-done, bf16[8192,128]{1,0:T(8,128)(2,1)} %bitcast.3), custom_call_target="tpu_custom_call" | custom-call | tf_op jit(solution)/shard_map/lag_correlation/pallas_call | solution.py:437
  65.6 0.8 %store_results.1 = (bf16[1152,128]{1,0:T(8,128)(2,1)}, bf16[1152,128]{1,0:T(8,128)(2,1)}) custom-call(bf16[1152,128]{1,0:T(8,128)(2,1)S(1)} %get-tuple-element.6.near, bf16[1152,128]{1,0:T(8,128)(2,1)S(1)} %get-tuple-element.7.far), custom_call_target="tpu_custom_call" | custom-call | tf_op jit(solution)/shard_map/store_results/pallas_call | solution.py:477
Async XLA Ops:
  0.6 0.7 copy-start

commit v4 on v3

--- a/solution.py
+++ b/solution.py
@@ -11,8 +11,9 @@
 LAGS = 2 * HL + 1
 CHUNKS = 8
 GROUPS = 3
-FIRST = 4
+FIRST = 6
 EARLY = 5
+BEFORE = 4
 VMEM_LIMIT = 52 * 1024 * 1024
 
 
@@ -175,7 +176,7 @@
     pl.semaphore_wait(barrier, expected)
 
     def far_copy(c):
-        sent = far_send.at[lax.div(c, FIRST)]
+        sent = far_send.at[jnp.where(c < FIRST, 0, 1)]
         return remote(own.at[part(c)], far.at[part(c)], sent, far_recv.at[c], across)
 
     def near_copy(c):
@@ -188,7 +189,7 @@
         return remote(far.at[part(c)], extra.at[part(c)], relay_send, extra_recv.at[c], half)
 
     def far_sent(group):
-        span = pl.ds(group * FIRST * size, FIRST * size)
+        span = pl.ds(0, FIRST * size) if group == 0 else pl.ds(FIRST * size, rows - FIRST * size)
         remote(
             own.at[span], far.at[span], far_send.at[group], far_recv.at[0], across
         ).wait_send()
@@ -284,30 +285,76 @@
         relay_to_extra(c).wait_recv()
         add(extra_acc, extra, c)
 
-    @pl.loop(0, CHUNKS - 1)
-    def _(c):
-        @pl.when(takes_far)
-        def _():
-            far_wait(c)
-            add(far_acc, far, c)
-
-        @pl.when(jnp.logical_and(c > 0, near_early))
-        def _():
-            near_step(c - 1)
-
-    @pl.when(near_early)
-    def _():
-        near_step(CHUNKS - 2)
-        near_step(CHUNKS - 1)
+    def xret_copy():
+        return remote(extra_buf, near_ret, xret_send, xret_recv, half - 1)
 
     @pl.when(me == half)
     def _():
         @pl.loop(0, CHUNKS)
         def _(c):
             near_step(c)
+
+            @pl.when(c < CHUNKS - 1)
+            def _():
+                add(far_acc, far, c)
+
             extra_step(c)
 
         extra_buf[...] = extra_acc[...].astype(jnp.bfloat16)
+        xret_copy().start()
+
+    def free(target):
+        pl.semaphore_signal(
+            mate_sent, inc=1, device_id={"chan": target}, device_id_type=pl.DeviceIdType.MESH
+        )
+
+    near_sender = jnp.logical_and(sends_far, near_early)
+
+    @pl.when(near_sender)
+    def _():
+        @pl.loop(0, BEFORE)
+        def _(c):
+            near_step(c)
+
+    @pl.when(sends_far)
+    def _():
+        @pl.when(me != half - 1)
+        def _():
+            far_sent(0)
+
+        far_sent(1)
+
+        @pl.when(mixed)
+        def _():
+            free(mate)
+
+        @pl.when(me == n - 5)
+        def _():
+            free(n - 1)
+
+    @pl.when(near_sender)
+    def _():
+        @pl.loop(BEFORE, CHUNKS)
+        def _(c):
+            near_step(c)
+
+    near_taker = jnp.logical_and(takes_far, near_early)
+
+    @pl.loop(0, CHUNKS - 1)
+    def _(c):
+        @pl.when(jnp.logical_and(takes_far, me != half))
+        def _():
+            far_wait(c)
+            add(far_acc, far, c)
+
+        @pl.when(jnp.logical_and(c > 0, near_taker))
+        def _():
+            near_step(c - 1)
+
+    @pl.when(near_taker)
+    def _():
+        near_step(CHUNKS - 2)
+        near_step(CHUNKS - 1)
 
     @pl.when(me == n - 1)
     def _():
@@ -321,9 +368,6 @@
     def ret_copy(g):
         span = pl.ds(g * band, band)
         return remote(far_out.at[span], far_ret.at[span], ret_send.at[g], ret_recv.at[g], across)
-
-    def xret_copy():
-        return remote(extra_buf, near_ret, xret_send, xret_recv, half - 1)
 
     @pl.when(takes_far)
     def _():
@@ -342,10 +386,6 @@
             ).astype(jnp.bfloat16)
             ret_copy(g).start()
 
-    @pl.when(me == half)
-    def _():
-        xret_copy().start()
-
     @pl.when(me == n - 1)
     def _():
         @pl.loop(EARLY, CHUNKS)
@@ -355,27 +395,6 @@
     @pl.when(near_here)
     def _():
         near_out[...] = near_acc[...].astype(jnp.bfloat16)
-
-    def free(target):
-        pl.semaphore_signal(
-            mate_sent, inc=1, device_id={"chan": target}, device_id_type=pl.DeviceIdType.MESH
-        )
-
-    @pl.when(sends_far)
-    def _():
-        @pl.when(me != half - 1)
-        def _():
-            far_sent(0)
-
-        far_sent(1)
-
-        @pl.when(mixed)
-        def _():
-            free(mate)
-
-        @pl.when(me == n - 5)
-        def _():
-            free(n - 1)
 
     def flip(src, dst, lag):
         tile = src[pl.ds((LAGS - 1 - lag) * chan, chan), :].astype(jnp.float32)
@@ -458,7 +477,7 @@
             dma((CHUNKS + 1,)),
             dma(()),
             dma((CHUNKS,)),
-            dma((CHUNKS // FIRST,)),
+            dma((2,)),
             dma((CHUNKS,)),
             dma(()),
             dma((CHUNKS,)),

time: 66.6 us -> 61.4 us (0.922)
  the two profiles are of different devices: /device:TPU:13 before, /device:TPU:8 now
where the time goes in v4:
time: 61.4 us; the launch traced here: 61.2 us
  Pallas kernels  59.9 us (98%)
  local copies, waits for them, and re-layouts  0.65 us (1%)
  between operations  0.65 us (1%)
    pallas_call x1, Pallas kernels, local(): pl.pallas_call(lambda *refs: kernel(n, windows, *refs), out_shape=(out, o...  59.1 us

profile of v4, /device:TPU:8, one launch (start us, length us, event | category | flops | bytes accessed | tf_op | source)
XLA Modules:
  0.0 61.2 jit_solution(2019385924760435071)
XLA Ops:
  0.6 0.0 copy-start
  0.6 0.6 %copy-done = s32[1,4]{1,0:T(1,128)S(1)} copy-done((s32[1,4]{1,0:T(1,128)S(1)}, s32[1,4]{1,0:T(1,128)}, u32[]{:S(2)}) %copy-start) | copy-done | bytes 40
  1.3 59.1 %lag_correlation.1 = (bf16[1152,128]{1,0:T(8,128)(2,1)S(1)}, bf16[1152,128]{1,0:T(8,128)(2,1)S(1)}) custom-call(s32[1,4]{1,0:T(1,128)S(1)} %copy-done, bf16[8192,128]{1,0:T(8,128)(2,1)} %bitcast.3), custom_call_target="tpu_custom_call" | custom-call | tf_op jit(solution)/shard_map/lag_correlation/pallas_call | solution.py:456
  60.4 0.8 %store_results.1 = (bf16[1152,128]{1,0:T(8,128)(2,1)}, bf16[1152,128]{1,0:T(8,128)(2,1)}) custom-call(bf16[1152,128]{1,0:T(8,128)(2,1)S(1)} %get-tuple-element.6.near, bf16[1152,128]{1,0:T(8,128)(2,1)S(1)} %get-tuple-element.7.far), custom_call_target="tpu_custom_call" | custom-call | tf_op jit(solution)/shard_map/store_results/pallas_call | solution.py:496
Async XLA Ops:
  0.6 0.7 %copy-start = (s32[1,4]{1,0:T(1,128)S(1)}, s32[1,4]{1,0:T(1,128)}, u32[]{:S(2)}) copy-start(s32[1,4]{1,0:T(1,128)} %refs_0_.1) | copy-start | bytes 52

commit v5 on v4

--- a/solution.py
+++ b/solution.py
@@ -11,9 +11,10 @@
 LAGS = 2 * HL + 1
 CHUNKS = 8
 GROUPS = 3
-FIRST = 6
-EARLY = 5
+FIRST = 7
+EARLY = 6
 BEFORE = 4
+SOON = 2
 VMEM_LIMIT = 52 * 1024 * 1024
 
 
@@ -298,10 +299,9 @@
             def _():
                 add(far_acc, far, c)
 
+        @pl.loop(0, SOON)
+        def _(c):
             extra_step(c)
-
-        extra_buf[...] = extra_acc[...].astype(jnp.bfloat16)
-        xret_copy().start()
 
     def free(target):
         pl.semaphore_signal(
@@ -312,7 +312,7 @@
 
     @pl.when(near_sender)
     def _():
-        @pl.loop(0, BEFORE)
+        @pl.loop(0, SOON)
         def _(c):
             near_step(c)
 
@@ -322,9 +322,13 @@
         def _():
             far_sent(0)
 
+        @pl.when(jnp.logical_and(mixed, jnp.logical_not(is_low)))
+        def _():
+            free(mate)
+
         far_sent(1)
 
-        @pl.when(mixed)
+        @pl.when(jnp.logical_and(mixed, is_low))
         def _():
             free(mate)
 
@@ -334,7 +338,7 @@
 
     @pl.when(near_sender)
     def _():
-        @pl.loop(BEFORE, CHUNKS)
+        @pl.loop(SOON, CHUNKS)
         def _(c):
             near_step(c)
 
@@ -342,19 +346,14 @@
 
     @pl.loop(0, CHUNKS - 1)
     def _(c):
+        @pl.when(jnp.logical_and(near_taker, c < BEFORE))
+        def _():
+            near_step(c)
+
         @pl.when(jnp.logical_and(takes_far, me != half))
         def _():
             far_wait(c)
             add(far_acc, far, c)
-
-        @pl.when(jnp.logical_and(c > 0, near_taker))
-        def _():
-            near_step(c - 1)
-
-    @pl.when(near_taker)
-    def _():
-        near_step(CHUNKS - 2)
-        near_step(CHUNKS - 1)
 
     @pl.when(me == n - 1)
     def _():
@@ -385,6 +384,21 @@
                 + jnp.dot(left[span, part(last)], right, preferred_element_type=jnp.float32)
             ).astype(jnp.bfloat16)
             ret_copy(g).start()
+
+    @pl.when(near_taker)
+    def _():
+        @pl.loop(BEFORE, CHUNKS)
+        def _(c):
+            near_step(c)
+
+    @pl.when(me == half)
+    def _():
+        @pl.loop(SOON, CHUNKS)
+        def _(c):
+            extra_step(c)
+
+        extra_buf[...] = extra_acc[...].astype(jnp.bfloat16)
+        xret_copy().start()
 
     @pl.when(me == n - 1)
     def _():
@@ -492,7 +506,7 @@
             collective_id=0, has_side_effects=True, vmem_limit_bytes=VMEM_LIMIT
         ),
         name="lag_correlation",
-    )(quality, spectra.reshape(rows, chan))
+    )(pltpu.with_memory_space_constraint(quality, pltpu.HBM), spectra.reshape(rows, chan))
     near, far = pl.pallas_call(
         store_results,
         out_shape=(out, out),

time: 61.4 us -> 60.4 us (0.984)
  the two profiles are of different devices: /device:TPU:8 before, /device:TPU:13 now
where the time goes in v5:
time: 60.4 us; the launch traced here: 60.3 us
  Pallas kernels  59.6 us (99%)
  between operations  0.64 us (1%)
    pallas_call x1, Pallas kernels, local(): pl.pallas_call(lambda *refs: kernel(n, windows, *refs), out_shape=(out, o...  58.8 us

profile of v5, /device:TPU:13, one launch (start us, length us, event | category | flops | bytes accessed | tf_op | source)
XLA Modules:
  0.0 60.3 jit_solution(304885373109457099)
XLA Ops:
  0.6 58.8 %lag_correlation.1 = (bf16[1152,128]{1,0:T(8,128)(2,1)S(1)}, bf16[1152,128]{1,0:T(8,128)(2,1)S(1)}) custom-call(s32[1,4]{1,0:T(1,128)} %refs_0_.1, bf16[8192,128]{1,0:T(8,128)(2,1)} %bitcast.3), custom_call_target="tpu_custom_call" | custom-call | tf_op jit(solution)/shard_map/lag_correlation/pallas_call | solution.py:470
  59.4 0.8 %store_results.1 = (bf16[1152,128]{1,0:T(8,128)(2,1)}, bf16[1152,128]{1,0:T(8,128)(2,1)}) custom-call(bf16[1152,128]{1,0:T(8,128)(2,1)S(1)} %get-tuple-element.6.near, bf16[1152,128]{1,0:T(8,128)(2,1)S(1)} %get-tuple-element.7.far), custom_call_target="tpu_custom_call" | custom-call | tf_op jit(solution)/shard_map/store_results/pallas_call | solution.py:510
